TPU v7x, 32 devices: a whole 2x2x4 slice. The times are simulated.
32 devices in a mesh: dp: 8 (over y, x, core), mp: 4 (over z).
Axes of the slice: x: 2, y: 2, z: 4, core: 2. Of those that a mesh axis runs over, the one named last changes fastest.
Arguments:
- image_latents: bfloat16 [16, 48, 3072], P('dp', None, 'mp'), may hold values from -6 to 6
- text_states: bfloat16 [112, 16, 3072], P('dp', None, 'mp'), may hold values from -6 to 6
- modulation: bfloat16 [112, 3, 3072], P('dp', None, 'mp'), may hold values from -2 to 2
- w_qkv: bfloat16 [3072, 3, 2048], P(None, None, 'mp'), may hold values from -0.109375 to 0.109375
- w_out: bfloat16 [2048, 3072], P('mp'), may hold values from -0.125 to 0.125
- q_gain: float32 [128], replicated, may hold values from 1.2 to 3
- k_gain: float32 [128], replicated, may hold values from 1.2 to 3
- branch_count: int32 [16], P('dp'), may hold values from 1 to 7, as said below
- branch_sign: int32 [112], P('dp'), may hold values from 0 to 1
- guide_weight: int32 [112], P('dp'), may hold values from 1 to 8
Outputs:
- prediction: bfloat16 [16, 48, 3072], P('dp', None, 'mp')
Inputs may be any that keep to these rules, and one draw needn't show every extreme that they name: `branch_count`: image i and image i + 8 have counts summing to 8, so the counts of all images sum to 64.
All inputs are finite; a program needn't handle non-finite values.
Results may differ from a plain program's by a relative error of at most 0.015.
Values may be sent and summed in bfloat16 or wider, within the bound.
A program may use at most 64 MiB of HBM per device.

v0:
```python
import jax
import jax.numpy as jnp
from jax import lax
from jax.sharding import PartitionSpec as P

epsilon = 1e-06


def rms_norm(values, gain):
    return values * lax.rsqrt(jnp.mean(values * values, axis=-1, keepdims=True) + epsilon) * gain


def single_block(sequence, modulation_rows, image_len, w_qkv, w_out, q_gain, k_gain):
    row_count, seq_len, local_width = sequence.shape
    full_width = local_width * lax.axis_size("mp")
    gathered, modulation_all = (
        lax.all_gather(sequence, "mp", axis=2, tiled=True),
        lax.all_gather(modulation_rows, "mp", axis=2, tiled=True),
    )
    states = gathered.astype(jnp.float32)
    row_mean = jnp.mean(states, axis=-1, keepdims=True)
    centered = states - row_mean
    spread = jnp.mean(centered * centered, axis=-1, keepdims=True)
    shift_rows = modulation_all[:, 0][:, None, :].astype(jnp.float32)
    scale_rows = modulation_all[:, 1][:, None, :].astype(jnp.float32)
    normed = (centered * lax.rsqrt(spread + epsilon) * (1.0 + scale_rows) + shift_rows).astype(
        jnp.bfloat16
    )
    head_dim = q_gain.shape[0]
    heads_here = w_out.shape[0] // head_dim
    projected = jnp.dot(
        normed.reshape(row_count * seq_len, full_width),
        w_qkv.reshape(full_width, 3 * heads_here * head_dim),
        preferred_element_type=jnp.float32,
    )
    projected = projected.reshape(row_count, seq_len, 3, heads_here, head_dim)
    queries = rms_norm(projected[:, :, 0], q_gain).astype(jnp.bfloat16)
    key_rows = rms_norm(projected[:, :, 1], k_gain).astype(jnp.bfloat16)
    value_rows = projected[:, :, 2].astype(jnp.bfloat16)
    scores = jnp.einsum(
        "rqhd,rkhd->rhqk", queries, key_rows, preferred_element_type=jnp.float32
    ) * head_dim ** (-0.5)
    attention_weights = jax.nn.softmax(scores, axis=-1).astype(jnp.bfloat16)
    attended = jnp.einsum(
        "rhqk,rkhd->rqhd", attention_weights, value_rows, preferred_element_type=jnp.float32
    ).astype(jnp.bfloat16)
    text_len = seq_len - image_len
    image_part = attended[:, text_len:].reshape(row_count * image_len, heads_here * head_dim)
    partial_value = jnp.dot(image_part, w_out, preferred_element_type=jnp.float32).reshape(
        row_count, image_len, full_width
    )
    out_rows = lax.psum_scatter(
        partial_value.astype(jnp.bfloat16), "mp", scatter_dimension=2, tiled=True
    ).astype(jnp.float32)
    gate_rows = modulation_rows[:, 2][:, None, :].astype(jnp.float32)
    return (sequence[:, text_len:].astype(jnp.float32) + gate_rows * out_rows).astype(jnp.bfloat16)


def on_device(
    image_latents,
    text_states,
    modulation,
    w_qkv,
    w_out,
    q_gain,
    k_gain,
    branch_count,
    branch_sign,
    guide_weight,
):
    image_count, image_len, local_width = image_latents.shape
    slot_count = text_states.shape[0]
    per_image = slot_count // image_count
    is_live = (jnp.arange(per_image, dtype=jnp.int32)[None, :] < branch_count[:, None]).reshape(-1)
    weights_live = jnp.where(is_live, guide_weight, 0).astype(jnp.float32)
    weight_total = jnp.sum(weights_live.reshape(image_count, per_image), axis=1)
    signed = jnp.where(
        is_live,
        (2 * branch_sign - 1).astype(jnp.float32)
        * weights_live
        / jnp.repeat(weight_total, per_image),
        0.0,
    )
    sequence = jnp.concatenate([text_states, jnp.repeat(image_latents, per_image, axis=0)], axis=1)
    returned = single_block(sequence, modulation, image_len, w_qkv, w_out, q_gain, k_gain)
    owner_image = jnp.arange(slot_count, dtype=jnp.int32) // per_image
    weights_table = (
        owner_image[None, :] == jnp.arange(image_count, dtype=jnp.int32)[:, None]
    ).astype(jnp.float32) * signed[None, :]
    prediction = jnp.einsum(
        "js,std->jtd", weights_table, returned.astype(jnp.float32), precision=lax.Precision.HIGHEST
    )
    return prediction.astype(jnp.bfloat16)


def solution(mesh):
    placed = (
        P("dp", None, "mp"),
        P("dp", None, "mp"),
        P("dp", None, "mp"),
        P(None, None, "mp"),
        P("mp", None),
        P(),
        P(),
        P("dp"),
        P("dp"),
        P("dp"),
    )
    return jax.shard_map(
        on_device, mesh=mesh, in_specs=placed, out_specs=P("dp", None, "mp"), check_vma=False
    )
```

profile of v0, /device:TPU:0, one launch (start us, length us, event | category | flops | bytes accessed | tf_op | source)
XLA Modules:
  0.0 235.7 jit_solution(667277126429270769)
XLA Ops:
  6.5 0.0 copy-start
  6.5 0.0 all-gather.2.cloned.1.call-start
  6.5 1.1 broadcast_in_dim.12
  7.7 2.2 pad_maximum_fusion
  9.9 0.0 all-gather.2.cloned.1.call-update
  9.9 0.0 copy-start.5
  9.9 0.0 reduce-scatter.2.cloned.1.call-start
  10.0 12.9 %copy.16 = bf16[3072,3,512]{0,2,1:T(8,128)(2,1)} copy(bf16[3072,3,512]{2,0,1:T(8,128)(2,1)} %param.13) | data formatting | bytes 18874368 | tf_op args[3]
  22.8 0.0 copy-done.5
  22.8 18.9 %all_gather.7 = bf16[14,3,3072]{2,0,1:T(8,128)(2,1)S(1)} all-gather(bf16[14,3,768]{2,0,1:T(8,128)(2,1)S(1)} %copy-done.5), channel_id=1, replica_groups=mesh['dp'=8,'mp'=4] {'mp'}, dimensions={2}, use_global_device_ids=true | all-gather | bytes 322560 | tf_op jit(solution)/shard_map/all_gather | solution.py:18
  41.8 78.0 %all-gather.2.cloned.1.call-done = bf16[14,64,3072]{2,1,0:T(8,128)(2,1)} async-done(((bf16[14,64,768]{2,1,0:T(8,128)(2,1)}), bf16[14,64,3072]{2,1,0:T(8,128)(2,1)}) %all-gather.2.cloned.1.call-update) | async-done | bytes 5505040 | tf_op jit(solution)/shard_map/all_gather | solution.py:17
  119.8 0.0 copy-start.1
  119.8 3.5 %convert_reduce_fusion = f32[14,64]{1,0:T(8,128)S(1)} fusion(bf16[14,64,3072]{2,1,0:T(8,128)(2,1)} %all-gather.2.cloned.1.call-done), kind=kLoop, calls=%fused_computation.2 | loop fusion | flops 5504128 | bytes 5508608 | tf_op jit(solution)/shard_map/reduce_sum | solution.py:21
  123.3 0.7 copy-done.1
  124.0 1.6 fusion.3
  125.6 12.8 %fusion.8 = f32[14,64,3,4,128]{4,1,3,2,0:T(8,128)S(1)} fusion(bf16[3,4,128,3072,1]{3,2,1,0,4:T(8,128)(2,1)} %bitcast.57, bf16[14,64,3072]{2,1,0:T(8,128)(2,1)S(1)} %copy-done.1, f32[14,3072]{1,0:T(8,128)S(1)} %fusion.33, f32[14,3072]{1,0:T(8,128)S(1)} %add_bitcast_fusion, f32[14,64]{1,0:T(8,128)S(1)} %add_rsqrt_fusion.2, ...), kind=kOutput, calls=%fused_computation.10 | convolution fusion | flops 8472231936 | bytes 20798464 | tf_op jit(solution)/shard_map/dot_general | solution.py:31
  138.3 0.0 copy-start.2
  138.3 0.0 copy-start.6
  138.4 0.0 copy-start.7
  138.4 1.1 multiply_reduce_fusion.1
  139.5 0.0 copy-done.6
  139.5 0.0 copy-done.7
  139.5 1.1 fusion.22
  140.6 0.1 copy-done.2
  140.7 0.0 copy-start.3
  140.7 1.3 copy-done.3
  142.0 0.6 fusion.49
  142.6 3.7 %fusion.16 = bf16[14,64,4,128]{3,1,2,0:T(8,128)(2,1)} fusion(f32[14,64,3,4,128]{4,1,3,2,0:T(8,128)} %copy-done.2, f32[14,4,64]{2,1,0:T(4,128)S(1)} %fusion.49, f32[14,4,64,64]{2,3,1,0:T(8,128)} %copy-done.3), kind=kOutput, calls=%fused_computation.31 | convolution fusion | flops 60100160 | bytes 3684352 | tf_op jit(solution)/shard_map/rhqk,rkhd->rqhd/dot_general | solution.py:44
  146.3 0.0 copy-done
  146.3 5.3 %convolution_convert_fusion = bf16[14,48,3072]{2,1,0:T(8,128)(2,1)} fusion(bf16[512,3072]{1,0:T(8,128)(2,1)S(1)} %copy-done, bf16[14,64,4,128]{3,1,2,0:T(8,128)(2,1)} %fusion.16), kind=kOutput, calls=%fused_computation.15 | convolution fusion | flops 2115993600 | bytes 7962624 | tf_op jit(solution)/shard_map/dot_general | solution.py:49
  151.7 0.0 copy-start.10
  151.7 0.0 copy-start.8
  151.7 0.0 copy-start.9
  151.7 0.0 copy-start.4
  151.7 0.0 reduce-scatter.2.cloned.1.call-update
  151.7 0.6 copy-done.10
  152.3 0.1 iota_compare_fusion
  152.4 0.1 lt.20
  152.5 0.0 copy-done.8
  152.5 0.1 reshape.73
  152.6 0.1 reduce_sum.54
  152.7 0.1 broadcast_in_dim.10
  152.8 0.1 reshape.74
  152.9 0.0 copy-done.9
  152.9 0.7 bitcast_convert_fusion
  153.6 72.3 %reduce-scatter.2.cloned.1.call-done = bf16[14,48,768]{2,1,0:T(8,128)(2,1)} async-done(((bf16[14,48,3072]{2,1,0:T(8,128)(2,1)}), bf16[14,48,768]{2,1,0:T(8,128)(2,1)}) %reduce-scatter.2.cloned.1.call-update) | async-done | bytes 1032208 | tf_op jit(solution)/shard_map/reduce_scatter | solution.py:52
  225.9 0.0 copy-done.4
  225.9 1.5 add_convert_fusion
  227.4 0.8 fusion.19
  228.2 0.7 copy.20
  (8 shorter events, 0.1 us)
Async XLA Ops:
  6.5 139.8 %copy-start = (bf16[512,3072]{1,0:T(8,128)(2,1)S(1)}, bf16[512,3072]{1,0:T(8,128)(2,1)}, u32[]{:S(2)}) copy-start(bf16[512,3072]{1,0:T(8,128)(2,1)} %param.14) | copy-start | bytes 9437188
  6.5 113.3 %all-gather.2.cloned.1.call-start = ((), (), s32[]{:S(2)}) async-start(), calls=%async_computation.1 | async-start | bytes 6881280 | tf_op jit(solution)/shard_map/all_gather | solution.py:17
  9.9 12.9 %copy-start.5 = (bf16[14,3,768]{2,0,1:T(8,128)(2,1)S(1)}, bf16[14,3,768]{2,0,1:T(8,128)(2,1)}, u32[]{:S(2)}) copy-start(bf16[14,3,768]{2,0,1:T(8,128)(2,1)} %param.12) | copy-start | bytes 193540
  9.9 216.0 %reduce-scatter.2.cloned.1.call-start = ((), (), s32[]{:S(2)}) async-start(), calls=%async_computation.2 | async-start | bytes 5160960 | tf_op jit(solution)/shard_map/reduce_scatter | solution.py:52
  119.8 4.2 %copy-start.1 = (bf16[14,64,3072]{2,1,0:T(8,128)(2,1)S(1)}, bf16[14,64,3072]{2,1,0:T(8,128)(2,1)}, u32[]{:S(2)}) copy-start(bf16[14,64,3072]{2,1,0:T(8,128)(2,1)} %all-gather.2.cloned.1.call-done) | copy-start | bytes 16515076
  138.3 2.4 %copy-start.2 = (f32[14,64,3,4,128]{4,1,3,2,0:T(8,128)}, f32[14,64,3,4,128]{4,1,3,2,0:T(8,128)S(1)}, u32[]{:S(2)}) copy-start(f32[14,64,3,4,128]{4,1,3,2,0:T(8,128)S(1)} %fusion.8) | copy-start | bytes 16515076
  138.3 1.1 copy-start.6
  138.4 1.1 copy-start.7
  140.7 1.3 copy-start.3
  151.7 0.7 copy-start.10
  151.7 0.8 copy-start.8
  151.7 1.2 copy-start.9
  151.7 74.3 %copy-start.4 = (bf16[2,48,768]{2,1,0:T(8,128)(2,1)S(1)}, bf16[2,48,768]{2,1,0:T(8,128)(2,1)}, u32[]{:S(2)}) copy-start(bf16[2,48,768]{2,1,0:T(8,128)(2,1)} %param.10) | copy-start | bytes 442372
Sparse Core Ops, SparseCore 0:
  10.0 109.7 all-gather.1
  151.8 74.0 reduce-scatter.1
where the time goes:
time: 236 us
  waiting for transfers between devices  150 us (64%)
  matrix products  23.7 us (10%)
  blocking collectives  18.9 us (8%)
  local copies, waits for them, and re-layouts  17.7 us (8%)
  between operations  13.5 us (6%)
  other arithmetic  11.4 us (5%)
    all_gather x1, waiting for transfers between devices, single_block(): lax.all_gather(sequence, 'mp', axis=2, tiled=True)  78 us
    reduce_scatter x1, waiting for transfers between devices, single_block(): lax.psum_scatter(partial_value.astype(jnp.bfloat16), 'mp', scatter_dimens...  72.3 us
    all_gather x1, blocking collectives, single_block(): lax.all_gather(modulation_rows, 'mp', axis=2, tiled=True)  18.9 us
    unnamed x23, local copies, waits for them, and re-layouts  15.5 us
    dot_general x1, matrix products, single_block(): jnp.dot(normed.reshape(row_count * seq_len, full_width), w_qkv.reshape(fu...  12.8 us
    dot_general x1, matrix products, single_block(): jnp.dot(image_part, w_out, preferred_element_type=jnp.float32)  5.33 us
  transfers between devices with their start and end apart: 2, of which 2 were waited for; matrix products, arithmetic and copies ran while one was open for 6% of the time, Pallas kernels for 0%

commit v1 on v0

v1 whole, which is shorter than its diff:
```python
import functools

import jax
import jax.numpy as jnp
from jax import lax
from jax.experimental import pallas as pl
from jax.experimental.pallas import tpu as pltpu
from jax.sharding import PartitionSpec as P

EPS = 1e-06
MESH = pl.DeviceIdType.MESH
F32 = jnp.float32
BF16 = jnp.bfloat16


def kernel(
    n, dp, per_image,
    cnt_ref, sgn_ref, gw_ref, img_ref, txt_ref, mod_ref, qg_ref, kg_ref, w_hbm, wo_hbm,
    out_ref,
    w_v, wo_v, ximg, xhat, mod_x, mod_y, mod_g, txt_y, txt_g, coef_x, coef_y,
    nimg, ntxt, q_s, k_s, v_s, att, acc, ysend, yrecv, rsend, rrecv,
    w_sem, zi_s, zi_r, zm_s, zm_r, zt_s, zt_r, yt_s, yt_r, yi_s, yi_r, yo_s, yo_r, zo_s, zo_r,
):
    me = lax.axis_index("mp")
    mine = lax.axis_index("dp")
    partner = lax.rem(mine + dp // 2, dp)
    images, img_len, width = img_ref.shape
    txt_len = txt_ref.shape[1]
    half = (per_image + 1) // 2
    extra = per_image - half
    full = n * width
    heads, hd = q_s.shape[1], q_s.shape[3]
    rows = half * img_len
    items = images * half

    weight_copies = [
        pltpu.make_async_copy(w_hbm.at[t], w_v.at[t], w_sem.at[t]) for t in range(3)
    ] + [
        pltpu.make_async_copy(
            wo_hbm.at[:, pl.ds(o * width, width)], wo_v.at[o], w_sem.at[3 + o]
        )
        for o in range(n)
    ]
    for c in weight_copies:
        c.start()

    def peer(d):
        return lax.rem(me + d, n)

    def source(d):
        return lax.rem(me - d + n, n)

    barrier = pltpu.get_barrier_semaphore()
    for d in range(1, n):
        pl.semaphore_signal(barrier, inc=1, device_id={"mp": peer(d)}, device_id_type=MESH)
    pl.semaphore_signal(barrier, inc=1, device_id={"dp": partner}, device_id_type=MESH)

    slots = images * per_image
    row_at = lax.broadcasted_iota(jnp.int32, coef_x.shape, 0)
    top = jnp.zeros(coef_x.shape, jnp.int32)
    low = jnp.ones(coef_x.shape, jnp.int32)
    for i in range(images):
        total = jnp.int32(0)
        for b in range(per_image):
            s = i * per_image + b
            live = jnp.where(b < cnt_ref[i], gw_ref[s], 0)
            total = total + live
            top = jnp.where(row_at == s, (2 * sgn_ref[s] - 1) * live, top)
        inside = (row_at >= i * per_image) & (row_at < (i + 1) * per_image)
        low = jnp.where(inside, total, low)
    coef_x[...] = top.astype(F32) / low.astype(F32)
    own_mod = [mod_ref[t].astype(F32) for t in range(3)]
    pieces = []
    for t in range(3):
        for i in range(images):
            first = i * per_image + half
            pieces.append(own_mod[t][first : first + extra])
        pieces.append(jnp.zeros((items - images * extra, width), F32))
    pieces.append(jnp.zeros((mod_x.shape[0] - 3 * items, width), F32))
    mod_x[...] = jnp.concatenate(pieces, axis=0).astype(BF16)

    pl.semaphore_wait(barrier, n)

    def to_peer(src, dst, send, recv, d):
        return pltpu.make_async_remote_copy(
            src_ref=src, dst_ref=dst, send_sem=send.at[d - 1], recv_sem=recv.at[d - 1],
            device_id={"mp": peer(d)}, device_id_type=MESH,
        )

    def to_partner(src, dst, send, recv):
        return pltpu.make_async_remote_copy(
            src_ref=src, dst_ref=dst, send_sem=send, recv_sem=recv,
            device_id={"dp": partner}, device_id_type=MESH,
        )

    zi = [to_peer(img_ref, ximg.at[0, me], zi_s, zi_r, d) for d in range(1, n)]
    yt = [to_partner(mod_x, mod_y, yt_s.at[0], yt_r.at[0])]
    for i in range(images):
        yt.append(
            to_partner(
                txt_ref.at[pl.ds(i * per_image + half, extra)], txt_y.at[i],
                yt_s.at[1 + i], yt_r.at[1 + i],
            )
        )
    yt.append(to_partner(coef_x, coef_y, yt_s.at[1 + images], yt_r.at[1 + images]))
    yi = [to_partner(img_ref, ximg.at[1, me], yi_s.at[0], yi_r.at[0])]
    for c in yt:
        c.start()
    for c in zi:
        c.start()
    yi[0].start()
    ximg[0, me] = img_ref[...]

    yt[0].wait_recv()
    got = mod_y[...].astype(F32)
    pieces = []
    for t in range(3):
        for i in range(images):
            for k in range(half):
                s = i * per_image + k
                row = own_mod[t][s : s + 1]
                if k > 0:
                    r = t * items + i * extra + extra - k
                    row = jnp.where(cnt_ref[i] > k, row, got[r : r + 1])
                pieces.append(row)
    pieces.append(jnp.zeros((mod_g.shape[1] - 3 * items, width), F32))
    mod_g[me] = jnp.concatenate(pieces, axis=0).astype(BF16)
    zm = [to_peer(mod_g.at[me], mod_g.at[me], zm_s, zm_r, d) for d in range(1, n)]
    for c in zm:
        c.start()
    zt = []
    for i in range(images):
        yt[1 + i].wait_recv()
        for k in range(half):
            own = txt_ref[i * per_image + k]
            if k > 0:
                own = jnp.where(
                    cnt_ref[i] > k, own.astype(F32), txt_y[i, extra - k].astype(F32)
                ).astype(BF16)
            txt_g[i, me, pl.ds(k * txt_len, txt_len), :] = own
        zt.append(
            [
                to_peer(txt_g.at[i, me], txt_g.at[i, me], zt_s.at[i], zt_r.at[i], d)
                for d in range(1, n)
            ]
        )
        for c in zt[i]:
            c.start()

    for d in range(1, n):
        zi[d - 1].wait_recv()
        o = source(d)
        c = to_partner(ximg.at[0, o], ximg.at[1, o], yi_s.at[d], yi_r.at[d])
        c.start()
        yi.append(c)

    def normalise(parts):
        mean = sum(jnp.sum(p, axis=-1, keepdims=True) for p in parts) * (1.0 / full)
        parts = [p - mean for p in parts]
        var = sum(jnp.sum(p * p, axis=-1, keepdims=True) for p in parts) * (1.0 / full)
        scale = lax.rsqrt(var + EPS)
        return [p * scale for p in parts]

    def image_hat(who):
        for i in range(images):
            parts = normalise([ximg[who, o, i].astype(F32) for o in range(n)])
            for o in range(n):
                xhat[who, i, o] = parts[o]

    image_hat(0)
    for c in zm:
        c.wait_recv()
    for c in yi:
        c.wait_recv()
    image_hat(1)

    for o in range(n):
        mods = mod_g[o].astype(F32)
        for i in range(images):
            for k in range(half):
                p = i * half + k
                who = jnp.where(cnt_ref[i] > k, 0, 1)
                hat = xhat[who, i, o]
                value = hat * (1.0 + mods[items + p : items + p + 1]) + mods[p : p + 1]
                nimg[pl.ds(p * img_len, img_len), pl.ds(o * width, width)] = value.astype(BF16)

    def rms(values, gain):
        mean = jnp.mean(values * values, axis=-1, keepdims=True)
        return values * lax.rsqrt(mean + EPS) * gain

    q_gain, k_gain = qg_ref[...], kg_ref[...]
    for t in range(3):
        weight_copies[t].wait()
        made = jnp.dot(nimg[...], w_v[t], preferred_element_type=F32)
        for h in range(heads):
            part = made[:, h * hd : (h + 1) * hd]
            if t == 0:
                part = rms(part, q_gain)
            if t == 1:
                part = rms(part, k_gain)
            part = part.astype(BF16)
            for i in range(images):
                (q_s, k_s, v_s)[t][i, h, pl.ds(0, rows), :] = part[i * rows : (i + 1) * rows]

    keys = half * (img_len + txt_len)
    q_row = lax.broadcasted_iota(jnp.int32, (rows, keys), 0)
    k_col = lax.broadcasted_iota(jnp.int32, (rows, keys), 1)
    same = jnp.zeros((rows, keys), jnp.bool_)
    for k in range(half):
        in_q = (q_row >= k * img_len) & (q_row < (k + 1) * img_len)
        in_img = (k_col >= k * img_len) & (k_col < (k + 1) * img_len)
        first = rows + k * txt_len
        in_txt = (k_col >= first) & (k_col < first + txt_len)
        same = same | (in_q & (in_img | in_txt))
    bias = jnp.where(same, 0.0, -1e30)

    yt[1 + images].wait_recv()
    for c in weight_copies[3:]:
        c.wait()

    def wide(row):
        return jnp.concatenate([row] * (width // row.shape[1]), axis=1)

    order = list(range(1, n)) + [0]
    yo = []
    for i in range(images):
        for c in zt[i]:
            c.wait_recv()
        parts = normalise([txt_g[i, o].astype(F32) for o in range(n)])
        for o in range(n):
            mods = mod_g[o].astype(F32)
            for k in range(half):
                p = i * half + k
                value = parts[o][k * txt_len : (k + 1) * txt_len]
                value = value * (1.0 + mods[items + p : items + p + 1]) + mods[p : p + 1]
                ntxt[pl.ds(k * txt_len, txt_len), pl.ds(o * width, width)] = value.astype(BF16)
        for t in (1, 2):
            made = jnp.dot(ntxt[...], w_v[t], preferred_element_type=F32)
            for h in range(heads):
                part = made[:, h * hd : (h + 1) * hd]
                if t == 1:
                    part = rms(part, k_gain)
                (k_s if t == 1 else v_s)[i, h, pl.ds(rows, half * txt_len), :] = part.astype(BF16)
        for h in range(heads):
            scores = lax.dot_general(
                q_s[i, h], k_s[i, h], (((1,), (1,)), ((), ())), preferred_element_type=F32
            ) * hd ** (-0.5) + bias
            powers = jnp.exp(scores - jnp.max(scores, axis=-1, keepdims=True))
            probs = powers / jnp.sum(powers, axis=-1, keepdims=True)
            att[:, pl.ds(h * hd, hd)] = jnp.dot(
                probs.astype(BF16), v_s[i, h], preferred_element_type=F32
            ).astype(BF16)
        sent = []
        for d in order:
            o = peer(d)
            part = jnp.dot(att[...], wo_v[o], preferred_element_type=F32).astype(BF16).astype(F32)
            mods = mod_g[o].astype(F32)
            own_sum = jnp.zeros((img_len, width), F32)
            far_sum = jnp.zeros((img_len, width), F32)
            for k in range(half):
                g = 2 * items + i * half + k
                term = part[k * img_len : (k + 1) * img_len] * mods[g : g + 1]
                s = i * per_image + k
                own_sum = own_sum + term * wide(coef_x[s : s + 1, :])
                if k > 0:
                    s = i * per_image + per_image - k
                    far_sum = far_sum + term * wide(coef_y[s : s + 1, :])
            acc[i, o] = own_sum
            ysend[i, o] = far_sum.astype(BF16)
            c = to_partner(ysend.at[i, o], yrecv.at[i, o], yo_s.at[i, d], yo_r.at[i, d])
            c.start()
            sent.append(c)
        yo.append(sent)

    zo = []
    for i in range(images):
        sent = []
        for at, d in enumerate(order):
            o = peer(d)
            yo[i][at].wait_recv()
            value = acc[i, o] + yrecv[i, o].astype(F32)
            if d == 0:
                acc[i, o] = value
                continue
            rsend[i, o] = value.astype(BF16)
            c = to_peer(rsend.at[i, o], rrecv.at[i, me], zo_s.at[i], zo_r.at[i], d)
            c.start()
            sent.append(c)
        zo.append(sent)

    for i in range(images):
        weight = jnp.zeros((1, coef_x.shape[1]), F32)
        for b in range(per_image):
            s = i * per_image + b
            weight = weight + coef_x[s : s + 1, :]
        value = acc[i, me] + img_ref[i].astype(F32) * wide(weight)
        for d in range(1, n):
            zo[i][d - 1].wait_recv()
            value = value + rrecv[i, source(d)].astype(F32)
        out_ref[i] = value.astype(BF16)

    for group in [zi, zm, yt, yi] + zt + yo + zo:
        for c in group:
            c.wait_send()


def on_device(
    n, dp,
    image_latents, text_states, modulation, w_qkv, w_out, q_gain, k_gain,
    branch_count, branch_sign, guide_weight,
):
    images, img_len, width = image_latents.shape
    slots, txt_len, _ = text_states.shape
    per_image = slots // images
    half = (per_image + 1) // 2
    extra = per_image - half
    full = n * width
    hd = q_gain.shape[0]
    inner = w_out.shape[0]
    heads = inner // hd
    rows = half * img_len
    keys = half * (img_len + txt_len)
    mod_rows = -(-3 * images * half // 16) * 16
    coef_rows = -(-slots // 16) * 16
    vmem = pl.BlockSpec(memory_space=pltpu.VMEM)
    smem = pl.BlockSpec(memory_space=pltpu.SMEM)
    hbm = pl.BlockSpec(memory_space=pl.ANY)
    dma = pltpu.SemaphoreType.DMA
    return pl.pallas_call(
        functools.partial(kernel, n, dp, per_image),
        out_shape=jax.ShapeDtypeStruct(image_latents.shape, BF16),
        in_specs=[smem] * 3 + [vmem] * 5 + [hbm] * 2,
        out_specs=vmem,
        scratch_shapes=[
            pltpu.VMEM((3, full, inner), BF16),
            pltpu.VMEM((n, inner, width), BF16),
            pltpu.VMEM((2, n, images, img_len, width), BF16),
            pltpu.VMEM((2, images, n, img_len, width), F32),
            pltpu.VMEM((mod_rows, width), BF16),
            pltpu.VMEM((mod_rows, width), BF16),
            pltpu.VMEM((n, mod_rows, width), BF16),
            pltpu.VMEM((images, extra, txt_len, width), BF16),
            pltpu.VMEM((images, n, half * txt_len, width), BF16),
            pltpu.VMEM((coef_rows, 128), F32),
            pltpu.VMEM((coef_rows, 128), F32),
            pltpu.VMEM((images * rows, full), BF16),
            pltpu.VMEM((half * txt_len, full), BF16),
            pltpu.VMEM((images, heads, rows, hd), BF16),
            pltpu.VMEM((images, heads, keys, hd), BF16),
            pltpu.VMEM((images, heads, keys, hd), BF16),
            pltpu.VMEM((rows, inner), BF16),
            pltpu.VMEM((images, n, img_len, width), F32),
            pltpu.VMEM((images, n, img_len, width), BF16),
            pltpu.VMEM((images, n, img_len, width), BF16),
            pltpu.VMEM((images, n, img_len, width), BF16),
            pltpu.VMEM((images, n, img_len, width), BF16),
            dma((3 + n,)),
            dma((n - 1,)), dma((n - 1,)),
            dma((n - 1,)), dma((n - 1,)),
            dma((images, n - 1)), dma((images, n - 1)),
            dma((2 + images,)), dma((2 + images,)),
            dma((n,)), dma((n,)),
            dma((images, n)), dma((images, n)),
            dma((images, n - 1)), dma((images, n - 1)),
        ],
        compiler_params=pltpu.CompilerParams(
            collective_id=0, has_side_effects=True, vmem_limit_bytes=56 * 1024 * 1024
        ),
    )(
        branch_count, branch_sign, guide_weight,
        image_latents, text_states, jnp.transpose(modulation, (1, 0, 2)),
        q_gain.reshape(1, hd), k_gain.reshape(1, hd),
        jnp.transpose(w_qkv, (1, 0, 2)), w_out,
    )


def solution(mesh):
    placed = (
        P("dp", None, "mp"),
        P("dp", None, "mp"),
        P("dp", None, "mp"),
        P(None, None, "mp"),
        P("mp", None),
        P(),
        P(),
        P("dp"),
        P("dp"),
        P("dp"),
    )
    return jax.shard_map(
        functools.partial(on_device, mesh.shape["mp"], mesh.shape["dp"]),
        mesh=mesh, in_specs=placed, out_specs=P("dp", None, "mp"), check_vma=False,
    )
```

time: 236 us -> 61.1 us (0.26)
  waiting for transfers between devices: 150 us -> 0 us
  Pallas kernels: 0 us -> 59.3 us
  matrix products: 23.7 us -> 0 us
  blocking collectives: 18.9 us -> 0 us
  local copies, waits for them, and re-layouts: 17.7 us -> 1.58 us
  between operations: 13.5 us -> 0.01 us
  other arithmetic: 11.4 us -> 0 us
    all_gather x1 -> x0, waiting for transfers between devices: 78 us -> none  [single_block(): lax.all_gather(sequence, 'mp', axis=2, tiled=True)]
    reduce_scatter x1 -> x0, waiting for transfers between devices: 72.3 us -> none  [single_block(): lax.psum_scatter(partial_value.astype(jnp.bfloat16), 'mp', scatter_dimens...]
    pallas_call x0 -> x1, Pallas kernels: none -> 59.3 us  [on_device(): pl.pallas_call(functools.partial(kernel, n, dp, per_image), out_shape=jax...]
    dot_general x5 -> x0, matrix products: 23.7 us -> none  [the longest x1 12.8 us: single_block(): jnp.dot(normed.reshape(row_count * seq_len, full_width), w_qkv.reshape(fu...]
    all_gather x1 -> x0, blocking collectives: 18.9 us -> none  [single_block(): lax.all_gather(modulation_rows, 'mp', axis=2, tiled=True)]
    unnamed x23 -> x1, local copies, waits for them, and re-layouts: 15.5 us -> 1.58 us
    reduce_sum x4 -> x0, other arithmetic: 6.26 us -> none  [the longest x1 3.51 us: single_block(): row_mean = jnp.mean(states, axis=-1, keepdims=True)]
  transfers between devices with their start and end apart: 2 -> 0, of which waited for: 2 -> 0; matrix products, arithmetic and copies ran while one was open for 6% -> 0% of each run, Pallas kernels for 0% -> 0%
where the time goes in v1:
time: 61.1 us; the launch traced here: 60.9 us
  Pallas kernels  59.3 us (97%)
  local copies, waits for them, and re-layouts  1.58 us (3%)
    pallas_call x1, Pallas kernels, on_device(): pl.pallas_call(functools.partial(kernel, n, dp, per_image), out_shape=jax...  59.3 us
    unnamed x1, local copies, waits for them, and re-layouts  1.58 us

profile of v1, /device:TPU:0, one launch (start us, length us, event | category | flops | bytes accessed | tf_op | source)
XLA Modules:
  0.0 60.9 jit_solution(18026545748373726821)
XLA Ops:
  0.0 59.3 %shard_map.100 = bf16[2,48,768]{2,1,0:T(8,128)(2,1)} custom-call(s32[2]{0:T(128)} %cnt_ref.1, s32[14]{0:T(128)} %sgn_ref.1, s32[14]{0:T(128)} %gw_ref.1, bf16[2,48,768]{2,1,0:T(8,128)(2,1)} %img_ref.1, bf16[14,16,768]{2,1,0:T(8,128)(2,1)} %txt_ref.1, bf16[3,14,768]{2,1,0:T(8,128)(2,1)} %bitcast.5, f32[1,128]{1,0:T(1,128)} %bitcast.6, f32[1,128]{1,0:T(1,128)} %bitcast.7, ...), custom_call_target="tpu_custom_call" | custom-call | tf_op jit(solution)/shard_map/pallas_call | solution.py:329
  59.3 1.6 %copy.12 = bf16[2,48,768]{2,1,0:T(8,128)(2,1)} copy(bf16[2,48,768]{2,1,0:T(8,128)(2,1)} %shard_map.100) | data formatting | bytes 294912

commit v2 on v1

--- a/solution.py
+++ b/solution.py
@@ -93,7 +93,41 @@
             device_id={"dp": partner}, device_id_type=MESH,
         )
 
-    zi = [to_peer(img_ref, ximg.at[0, me], zi_s, zi_r, d) for d in range(1, n)]
+    def chain(ref_of, send, recv, way, s, first=None):
+        chunk = lax.rem(me - s + n, n) if way == 0 else lax.rem(me + s, n)
+        target = lax.rem(me + 1, n) if way == 0 else lax.rem(me + n - 1, n)
+        return pltpu.make_async_remote_copy(
+            src_ref=ref_of(chunk) if first is None or s > 0 else first,
+            dst_ref=ref_of(chunk), send_sem=send.at[way, s], recv_sem=recv.at[way, s],
+            device_id={"mp": target}, device_id_type=MESH,
+        )
+
+    def chain_start(s, *args):
+        pl.when((me >= s) & (me + 1 < n))(lambda: chain(*args[:3], 0, s, *args[3:]).start())
+        pl.when((me + s < n) & (me >= 1))(lambda: chain(*args[:3], 1, s, *args[3:]).start())
+
+    def chain_sent(s, *args):
+        pl.when((me >= s) & (me + 1 < n))(lambda: chain(*args[:3], 0, s, *args[3:]).wait_send())
+        pl.when((me + s < n) & (me >= 1))(lambda: chain(*args[:3], 1, s, *args[3:]).wait_send())
+
+    def arrived(way, s):
+        return me >= s + 1 if way == 0 else me + s + 1 < n
+
+    def chain_wait(s, *args):
+        for way in range(2):
+            pl.when(arrived(way, s))(
+                lambda way=way: chain(*args[:3], way, s, *args[3:]).wait_recv()
+            )
+
+    def near(way, s):
+        return lax.rem(me - s - 1 + n, n) if way == 0 else lax.rem(me + s + 1, n)
+
+    def pass_on(way, s):
+        o = near(way, s)
+        return to_partner(ximg.at[0, o], ximg.at[1, o], yi_s.at[way, s], yi_r.at[way, s])
+
+    img_chain = (lambda o: ximg.at[0, o], zi_s, zi_r, img_ref)
+    mod_chain = (lambda o: mod_g.at[o], zm_s, zm_r)
     yt = [to_partner(mod_x, mod_y, yt_s.at[0], yt_r.at[0])]
     for i in range(images):
         yt.append(
@@ -103,12 +137,10 @@
             )
         )
     yt.append(to_partner(coef_x, coef_y, yt_s.at[1 + images], yt_r.at[1 + images]))
-    yi = [to_partner(img_ref, ximg.at[1, me], yi_s.at[0], yi_r.at[0])]
+    yt.append(to_partner(img_ref, ximg.at[1, me], yt_s.at[2 + images], yt_r.at[2 + images]))
+    chain_start(0, *img_chain)
     for c in yt:
         c.start()
-    for c in zi:
-        c.start()
-    yi[0].start()
     ximg[0, me] = img_ref[...]
 
     yt[0].wait_recv()
@@ -125,11 +157,10 @@
                 pieces.append(row)
     pieces.append(jnp.zeros((mod_g.shape[1] - 3 * items, width), F32))
     mod_g[me] = jnp.concatenate(pieces, axis=0).astype(BF16)
-    zm = [to_peer(mod_g.at[me], mod_g.at[me], zm_s, zm_r, d) for d in range(1, n)]
-    for c in zm:
-        c.start()
+    chain_start(0, *mod_chain)
     zt = []
-    for i in range(images):
+
+    def send_text(i):
         yt[1 + i].wait_recv()
         for k in range(half):
             own = txt_ref[i * per_image + k]
@@ -147,12 +178,18 @@
         for c in zt[i]:
             c.start()
 
-    for d in range(1, n):
-        zi[d - 1].wait_recv()
-        o = source(d)
-        c = to_partner(ximg.at[0, o], ximg.at[1, o], yi_s.at[d], yi_r.at[d])
-        c.start()
-        yi.append(c)
+    send_text(0)
+    for s in range(n - 1):
+        chain_wait(s, *img_chain)
+        if s + 1 < n - 1:
+            chain_start(s + 1, *img_chain)
+        for way in range(2):
+            pl.when(arrived(way, s))(lambda way=way, s=s: pass_on(way, s).start())
+        chain_wait(s, *mod_chain)
+        if s + 1 < n - 1:
+            chain_start(s + 1, *mod_chain)
+    for i in range(1, images):
+        send_text(i)
 
     def normalise(parts):
         mean = sum(jnp.sum(p, axis=-1, keepdims=True) for p in parts) * (1.0 / full)
@@ -168,10 +205,10 @@
                 xhat[who, i, o] = parts[o]
 
     image_hat(0)
-    for c in zm:
-        c.wait_recv()
-    for c in yi:
-        c.wait_recv()
+    yt[2 + images].wait_recv()
+    for s in range(n - 1):
+        for way in range(2):
+            pl.when(arrived(way, s))(lambda way=way, s=s: pass_on(way, s).wait_recv())
     image_hat(1)
 
     for o in range(n):
@@ -223,9 +260,28 @@
 
     order = list(range(1, n)) + [0]
     yo = []
+    zo = []
+
+    def reduce_image(i):
+        sent = []
+        for at, d in enumerate(order):
+            o = peer(d)
+            yo[i][at].wait_recv()
+            value = acc[i, o] + yrecv[i, o].astype(F32)
+            if d == 0:
+                acc[i, o] = value
+                continue
+            rsend[i, o] = value.astype(BF16)
+            c = to_peer(rsend.at[i, o], rrecv.at[i, me], zo_s.at[i], zo_r.at[i], d)
+            c.start()
+            sent.append(c)
+        zo.append(sent)
+
     for i in range(images):
         for c in zt[i]:
             c.wait_recv()
+        if i > 0:
+            reduce_image(i - 1)
         parts = normalise([txt_g[i, o].astype(F32) for o in range(n)])
         for o in range(n):
             mods = mod_g[o].astype(F32)
@@ -272,21 +328,7 @@
             sent.append(c)
         yo.append(sent)
 
-    zo = []
-    for i in range(images):
-        sent = []
-        for at, d in enumerate(order):
-            o = peer(d)
-            yo[i][at].wait_recv()
-            value = acc[i, o] + yrecv[i, o].astype(F32)
-            if d == 0:
-                acc[i, o] = value
-                continue
-            rsend[i, o] = value.astype(BF16)
-            c = to_peer(rsend.at[i, o], rrecv.at[i, me], zo_s.at[i], zo_r.at[i], d)
-            c.start()
-            sent.append(c)
-        zo.append(sent)
+    reduce_image(images - 1)
 
     for i in range(images):
         weight = jnp.zeros((1, coef_x.shape[1]), F32)
@@ -299,9 +341,14 @@
             value = value + rrecv[i, source(d)].astype(F32)
         out_ref[i] = value.astype(BF16)
 
-    for group in [zi, zm, yt, yi] + zt + yo + zo:
+    for group in [yt] + zt + yo + zo:
         for c in group:
             c.wait_send()
+    for s in range(n - 1):
+        chain_sent(s, *img_chain)
+        chain_sent(s, *mod_chain)
+        for way in range(2):
+            pl.when(arrived(way, s))(lambda way=way, s=s: pass_on(way, s).wait_send())
 
 
 def on_device(
@@ -355,11 +402,11 @@
             pltpu.VMEM((images, n, img_len, width), BF16),
             pltpu.VMEM((images, n, img_len, width), BF16),
             dma((3 + n,)),
-            dma((n - 1,)), dma((n - 1,)),
-            dma((n - 1,)), dma((n - 1,)),
+            dma((2, n - 1)), dma((2, n - 1)),
+            dma((2, n - 1)), dma((2, n - 1)),
             dma((images, n - 1)), dma((images, n - 1)),
-            dma((2 + images,)), dma((2 + images,)),
-            dma((n,)), dma((n,)),
+            dma((3 + images,)), dma((3 + images,)),
+            dma((2, n - 1)), dma((2, n - 1)),
             dma((images, n)), dma((images, n)),
             dma((images, n - 1)), dma((images, n - 1)),
         ],

time: 61.1 us -> 64.6 us (1.057)
  Pallas kernels: 59.3 us -> 62.9 us
    pallas_call x1, Pallas kernels: 59.3 us -> 62.9 us  [on_device(): pl.pallas_call(functools.partial(kernel, n, dp, per_image), out_shape=jax...]
where the time goes in v2:
time: 64.6 us; the launch traced here: 64.5 us
  Pallas kernels  62.9 us (97%)
  local copies, waits for them, and re-layouts  1.58 us (2%)
    pallas_call x1, Pallas kernels, on_device(): pl.pallas_call(functools.partial(kernel, n, dp, per_image), out_shape=jax...  62.9 us
    unnamed x1, local copies, waits for them, and re-layouts  1.58 us

profile of v2, /device:TPU:0, one launch (start us, length us, event | category | flops | bytes accessed | tf_op | source)
XLA Modules:
  0.0 64.5 jit_solution(5557634031528710198)
XLA Ops:
  0.0 62.9 %shard_map.100 = bf16[2,48,768]{2,1,0:T(8,128)(2,1)} custom-call(s32[2]{0:T(128)} %cnt_ref.1, s32[14]{0:T(128)} %sgn_ref.1, s32[14]{0:T(128)} %gw_ref.1, bf16[2,48,768]{2,1,0:T(8,128)(2,1)} %img_ref.1, bf16[14,16,768]{2,1,0:T(8,128)(2,1)} %txt_ref.1, bf16[3,14,768]{2,1,0:T(8,128)(2,1)} %bitcast.5, f32[1,128]{1,0:T(1,128)} %bitcast.6, f32[1,128]{1,0:T(1,128)} %bitcast.7, ...), custom_call_target="tpu_custom_call" | custom-call | tf_op jit(solution)/shard_map/pallas_call | solution.py:376
  62.9 1.6 %copy.12 = bf16[2,48,768]{2,1,0:T(8,128)(2,1)} copy(bf16[2,48,768]{2,1,0:T(8,128)(2,1)} %shard_map.100) | data formatting | bytes 294912

commit v3 on v1

--- a/solution.py
+++ b/solution.py
@@ -45,10 +45,10 @@
         c.start()
 
     def peer(d):
-        return lax.rem(me + d, n)
-
-    def source(d):
-        return lax.rem(me - d + n, n)
+        place = me
+        for bit in (1 << b for b in range(d.bit_length()) if d >> b & 1):
+            place = place + bit * (1 - 2 * lax.rem(lax.div(me, bit), 2))
+        return place
 
     barrier = pltpu.get_barrier_semaphore()
     for d in range(1, n):
@@ -144,12 +144,12 @@
                 for d in range(1, n)
             ]
         )
-        for c in zt[i]:
+        for c in reversed(zt[i]):
             c.start()
 
     for d in range(1, n):
         zi[d - 1].wait_recv()
-        o = source(d)
+        o = peer(d)
         c = to_partner(ximg.at[0, o], ximg.at[1, o], yi_s.at[d], yi_r.at[d])
         c.start()
         yi.append(c)
@@ -221,8 +221,23 @@
     def wide(row):
         return jnp.concatenate([row] * (width // row.shape[1]), axis=1)
 
-    order = list(range(1, n)) + [0]
+    order = list(range(n - 1, -1, -1))
     yo = []
+    zo = [[] for _ in range(images)]
+
+    def reduce_chunk(i, at):
+        d = order[at]
+        o = peer(d)
+        yo[i][at].wait_recv()
+        value = acc[i, o] + yrecv[i, o].astype(F32)
+        if d == 0:
+            acc[i, o] = value
+            return
+        rsend[i, o] = value.astype(BF16)
+        c = to_peer(rsend.at[i, o], rrecv.at[i, me], zo_s.at[i], zo_r.at[i], d)
+        c.start()
+        zo[i].append(c)
+
     for i in range(images):
         for c in zt[i]:
             c.wait_recv()
@@ -242,6 +257,9 @@
                     part = rms(part, k_gain)
                 (k_s if t == 1 else v_s)[i, h, pl.ds(rows, half * txt_len), :] = part.astype(BF16)
         for h in range(heads):
+            if i > 0:
+                for at in range(h * n // heads, (h + 1) * n // heads):
+                    reduce_chunk(i - 1, at)
             scores = lax.dot_general(
                 q_s[i, h], k_s[i, h], (((1,), (1,)), ((), ())), preferred_element_type=F32
             ) * hd ** (-0.5) + bias
@@ -272,21 +290,8 @@
             sent.append(c)
         yo.append(sent)
 
-    zo = []
-    for i in range(images):
-        sent = []
-        for at, d in enumerate(order):
-            o = peer(d)
-            yo[i][at].wait_recv()
-            value = acc[i, o] + yrecv[i, o].astype(F32)
-            if d == 0:
-                acc[i, o] = value
-                continue
-            rsend[i, o] = value.astype(BF16)
-            c = to_peer(rsend.at[i, o], rrecv.at[i, me], zo_s.at[i], zo_r.at[i], d)
-            c.start()
-            sent.append(c)
-        zo.append(sent)
+    for at in range(n):
+        reduce_chunk(images - 1, at)
 
     for i in range(images):
         weight = jnp.zeros((1, coef_x.shape[1]), F32)
@@ -295,8 +300,8 @@
             weight = weight + coef_x[s : s + 1, :]
         value = acc[i, me] + img_ref[i].astype(F32) * wide(weight)
         for d in range(1, n):
-            zo[i][d - 1].wait_recv()
-            value = value + rrecv[i, source(d)].astype(F32)
+            zo[i][order.index(d)].wait_recv()
+            value = value + rrecv[i, peer(d)].astype(F32)
         out_ref[i] = value.astype(BF16)
 
     for group in [zi, zm, yt, yi] + zt + yo + zo:

time: 61.1 us -> 64.6 us (1.057)
  Pallas kernels: 59.3 us -> 62.8 us
    pallas_call x1, Pallas kernels: 59.3 us -> 62.8 us  [on_device(): pl.pallas_call(functools.partial(kernel, n, dp, per_image), out_shape=jax...]
where the time goes in v3:
time: 64.6 us; the launch traced here: 64.4 us
  Pallas kernels  62.8 us (97%)
  local copies, waits for them, and re-layouts  1.58 us (2%)
    pallas_call x1, Pallas kernels, on_device(): pl.pallas_call(functools.partial(kernel, n, dp, per_image), out_shape=jax...  62.8 us
    unnamed x1, local copies, waits for them, and re-layouts  1.58 us

profile of v3, /device:TPU:0, one launch (start us, length us, event | category | flops | bytes accessed | tf_op | source)
XLA Modules:
  0.0 64.4 jit_solution(17347568396895533502)
XLA Ops:
  0.0 62.8 %shard_map.100 = bf16[2,48,768]{2,1,0:T(8,128)(2,1)} custom-call(s32[2]{0:T(128)} %cnt_ref.1, s32[14]{0:T(128)} %sgn_ref.1, s32[14]{0:T(128)} %gw_ref.1, bf16[2,48,768]{2,1,0:T(8,128)(2,1)} %img_ref.1, bf16[14,16,768]{2,1,0:T(8,128)(2,1)} %txt_ref.1, bf16[3,14,768]{2,1,0:T(8,128)(2,1)} %bitcast.5, f32[1,128]{1,0:T(1,128)} %bitcast.6, f32[1,128]{1,0:T(1,128)} %bitcast.7, ...), custom_call_target="tpu_custom_call" | custom-call | tf_op jit(solution)/shard_map/pallas_call | solution.py:334
  62.8 1.6 %copy.12 = bf16[2,48,768]{2,1,0:T(8,128)(2,1)} copy(bf16[2,48,768]{2,1,0:T(8,128)(2,1)} %shard_map.100) | data formatting | bytes 294912

commit v4 on v3

--- a/solution.py
+++ b/solution.py
@@ -248,18 +248,22 @@
                 p = i * half + k
                 value = parts[o][k * txt_len : (k + 1) * txt_len]
                 value = value * (1.0 + mods[items + p : items + p + 1]) + mods[p : p + 1]
-                ntxt[pl.ds(k * txt_len, txt_len), pl.ds(o * width, width)] = value.astype(BF16)
-        for t in (1, 2):
-            made = jnp.dot(ntxt[...], w_v[t], preferred_element_type=F32)
-            for h in range(heads):
-                part = made[:, h * hd : (h + 1) * hd]
-                if t == 1:
-                    part = rms(part, k_gain)
-                (k_s if t == 1 else v_s)[i, h, pl.ds(rows, half * txt_len), :] = part.astype(BF16)
+                ntxt[pl.ds(p * txt_len, txt_len), pl.ds(o * width, width)] = value.astype(BF16)
+    tail = half * txt_len
+    for t in (1, 2):
+        made = jnp.dot(ntxt[...], w_v[t], preferred_element_type=F32)
         for h in range(heads):
-            if i > 0:
-                for at in range(h * n // heads, (h + 1) * n // heads):
-                    reduce_chunk(i - 1, at)
+            part = made[:, h * hd : (h + 1) * hd]
+            if t == 1:
+                part = rms(part, k_gain)
+            part = part.astype(BF16)
+            for i in range(images):
+                (k_s if t == 1 else v_s)[i, h, pl.ds(rows, tail), :] = part[
+                    i * tail : (i + 1) * tail
+                ]
+
+    for i in range(images):
+        for h in range(heads):
             scores = lax.dot_general(
                 q_s[i, h], k_s[i, h], (((1,), (1,)), ((), ())), preferred_element_type=F32
             ) * hd ** (-0.5) + bias
@@ -269,7 +273,7 @@
                 probs.astype(BF16), v_s[i, h], preferred_element_type=F32
             ).astype(BF16)
         sent = []
-        for d in order:
+        for at, d in enumerate(order):
             o = peer(d)
             part = jnp.dot(att[...], wo_v[o], preferred_element_type=F32).astype(BF16).astype(F32)
             mods = mod_g[o].astype(F32)
@@ -288,6 +292,8 @@
             c = to_partner(ysend.at[i, o], yrecv.at[i, o], yo_s.at[i, d], yo_r.at[i, d])
             c.start()
             sent.append(c)
+            if i > 0:
+                reduce_chunk(i - 1, at)
         yo.append(sent)
 
     for at in range(n):
@@ -349,7 +355,7 @@
             pltpu.VMEM((coef_rows, 128), F32),
             pltpu.VMEM((coef_rows, 128), F32),
             pltpu.VMEM((images * rows, full), BF16),
-            pltpu.VMEM((half * txt_len, full), BF16),
+            pltpu.VMEM((images * half * txt_len, full), BF16),
             pltpu.VMEM((images, heads, rows, hd), BF16),
             pltpu.VMEM((images, heads, keys, hd), BF16),
             pltpu.VMEM((images, heads, keys, hd), BF16),

time: 64.6 us -> 61.9 us (0.958)
  Pallas kernels: 62.8 us -> 60.1 us
    pallas_call x1, Pallas kernels: 62.8 us -> 60.1 us  [on_device(): pl.pallas_call(functools.partial(kernel, n, dp, per_image), out_shape=jax...]
where the time goes in v4:
time: 61.9 us; the launch traced here: 61.7 us
  Pallas kernels  60.1 us (97%)
  local copies, waits for them, and re-layouts  1.58 us (3%)
    pallas_call x1, Pallas kernels, on_device(): pl.pallas_call(functools.partial(kernel, n, dp, per_image), out_shape=jax...  60.1 us
    unnamed x1, local copies, waits for them, and re-layouts  1.58 us

profile of v4, /device:TPU:0, one launch (start us, length us, event | category | flops | bytes accessed | tf_op | source)
XLA Modules:
  0.0 61.7 jit_solution(8521175014545479022)
XLA Ops:
  0.0 60.1 %shard_map.100 = bf16[2,48,768]{2,1,0:T(8,128)(2,1)} custom-call(s32[2]{0:T(128)} %cnt_ref.1, s32[14]{0:T(128)} %sgn_ref.1, s32[14]{0:T(128)} %gw_ref.1, bf16[2,48,768]{2,1,0:T(8,128)(2,1)} %img_ref.1, bf16[14,16,768]{2,1,0:T(8,128)(2,1)} %txt_ref.1, bf16[3,14,768]{2,1,0:T(8,128)(2,1)} %bitcast.5, f32[1,128]{1,0:T(1,128)} %bitcast.6, f32[1,128]{1,0:T(1,128)} %bitcast.7, ...), custom_call_target="tpu_custom_call" | custom-call | tf_op jit(solution)/shard_map/pallas_call | solution.py:340
  60.1 1.6 %copy.12 = bf16[2,48,768]{2,1,0:T(8,128)(2,1)} copy(bf16[2,48,768]{2,1,0:T(8,128)(2,1)} %shard_map.100) | data formatting | bytes 294912

commit v5 on v4

--- a/solution.py
+++ b/solution.py
@@ -45,10 +45,10 @@
         c.start()
 
     def peer(d):
-        place = me
-        for bit in (1 << b for b in range(d.bit_length()) if d >> b & 1):
-            place = place + bit * (1 - 2 * lax.rem(lax.div(me, bit), 2))
-        return place
+        return lax.rem(me + d, n)
+
+    def source(d):
+        return lax.rem(me - d + n, n)
 
     barrier = pltpu.get_barrier_semaphore()
     for d in range(1, n):
@@ -144,12 +144,12 @@
                 for d in range(1, n)
             ]
         )
-        for c in reversed(zt[i]):
+        for c in zt[i]:
             c.start()
 
     for d in range(1, n):
         zi[d - 1].wait_recv()
-        o = peer(d)
+        o = source(d)
         c = to_partner(ximg.at[0, o], ximg.at[1, o], yi_s.at[d], yi_r.at[d])
         c.start()
         yi.append(c)
@@ -221,7 +221,7 @@
     def wide(row):
         return jnp.concatenate([row] * (width // row.shape[1]), axis=1)
 
-    order = list(range(n - 1, -1, -1))
+    order = list(range(1, n)) + [0]
     yo = []
     zo = [[] for _ in range(images)]
 
@@ -307,7 +307,7 @@
         value = acc[i, me] + img_ref[i].astype(F32) * wide(weight)
         for d in range(1, n):
             zo[i][order.index(d)].wait_recv()
-            value = value + rrecv[i, peer(d)].astype(F32)
+            value = value + rrecv[i, source(d)].astype(F32)
         out_ref[i] = value.astype(BF16)
 
     for group in [zi, zm, yt, yi] + zt + yo + zo:

time: 61.9 us -> 63.3 us (1.023)
  Pallas kernels: 60.1 us -> 61.6 us
    pallas_call x1, Pallas kernels: 60.1 us -> 61.6 us  [on_device(): pl.pallas_call(functools.partial(kernel, n, dp, per_image), out_shape=jax...]
where the time goes in v5:
time: 63.3 us; the launch traced here: 63.2 us
  Pallas kernels  61.6 us (97%)
  local copies, waits for them, and re-layouts  1.58 us (2%)
    pallas_call x1, Pallas kernels, on_device(): pl.pallas_call(functools.partial(kernel, n, dp, per_image), out_shape=jax...  61.6 us
    unnamed x1, local copies, waits for them, and re-layouts  1.58 us

profile of v5, /device:TPU:0, one launch (start us, length us, event | category | flops | bytes accessed | tf_op | source)
XLA Modules:
  0.0 63.2 jit_solution(1222196593285182301)
XLA Ops:
  0.0 61.6 %shard_map.100 = bf16[2,48,768]{2,1,0:T(8,128)(2,1)} custom-call(s32[2]{0:T(128)} %cnt_ref.1, s32[14]{0:T(128)} %sgn_ref.1, s32[14]{0:T(128)} %gw_ref.1, bf16[2,48,768]{2,1,0:T(8,128)(2,1)} %img_ref.1, bf16[14,16,768]{2,1,0:T(8,128)(2,1)} %txt_ref.1, bf16[3,14,768]{2,1,0:T(8,128)(2,1)} %bitcast.5, f32[1,128]{1,0:T(1,128)} %bitcast.6, f32[1,128]{1,0:T(1,128)} %bitcast.7, ...), custom_call_target="tpu_custom_call" | custom-call | tf_op jit(solution)/shard_map/pallas_call | solution.py:340
  61.6 1.6 %copy.12 = bf16[2,48,768]{2,1,0:T(8,128)(2,1)} copy(bf16[2,48,768]{2,1,0:T(8,128)(2,1)} %shard_map.100) | data formatting | bytes 294912
